TPU v7x, 32 devices: a whole 2x2x4 slice. The times are simulated.
32 devices in a mesh: grp: 2 (over x), gx: 16 (over z, y, core).
Axes of the slice: x: 2, y: 2, z: 4, core: 2. Of those that a mesh axis runs over, the one named last changes fastest.
Arguments:
- saved_field: bfloat16 [128, 128, 512], P(('grp', 'gx')), parts along dimension 0, may hold values from -6 to 6
- right_side: float32 [128, 128, 512], P(('grp', 'gx')), parts along dimension 0, may hold values from -6 to 6
- face_x: float32 [128, 128, 512], P(('grp', 'gx')), parts along dimension 0, may hold values from 0.1 to 10
- face_y: float32 [128, 128, 512], P(('grp', 'gx')), parts along dimension 0, may hold values from 0.1 to 10
- face_z: float32 [128, 128, 512], P(('grp', 'gx')), parts along dimension 0, may hold values from 0.1 to 10
- cotangent: float32 [128, 128, 512], P(('grp', 'gx')), parts along dimension 0, may hold values from -6 to 6
Outputs:
- adjoint_field: float32 [128, 128, 512], P(('grp', 'gx')), parts along dimension 0
- grad_x: float32 [128, 128, 512], P(('grp', 'gx')), parts along dimension 0
- grad_y: float32 [128, 128, 512], P(('grp', 'gx')), parts along dimension 0
- grad_z: float32 [128, 128, 512], P(('grp', 'gx')), parts along dimension 0
There are 2 independent parts, one for each index of `grp`. A program takes and returns all parts, laid end to end along the dimension named above; each array names one. Nothing has to cross between parts.
All inputs are finite; a program needn't handle non-finite values.
Results may differ from a plain program's by a relative error of at most 0.0003.
Values sent between devices are 32-bit elements; how exact they have to be, the bound alone decides.
A program may use at most 64 MiB of HBM per device.

v0:
```python
import jax
import jax.numpy as jnp
from jax import lax
from jax.experimental import pallas as pl
from jax.experimental.pallas import tpu as pltpu
from jax.sharding import PartitionSpec as P

STEPS = 4
ROWS = 16
PAD = 8

spectrum_low = 0.25
spectrum_high = 2.05


def chebyshev(count):
    centre = (spectrum_high + spectrum_low) / 2.0
    half = (spectrum_high - spectrum_low) / 2.0
    ratio = centre / half
    rho_prev = 1.0 / ratio
    coefs = [(0.0, 1.0 / centre)]
    for index in range(1, count):
        rho_next = 1.0 / (2.0 * ratio - rho_prev)
        coefs.append((rho_next * rho_prev, 2.0 * rho_next / half))
        rho_prev = rho_next
    return coefs


def make_kernel(n, layers, ny, nz):
    coefs = chebyshev(STEPS)
    top = layers
    high = layers + 1
    last = STEPS - 1
    f32 = jnp.float32

    def kernel(saved_h, rhs_h, fx_h, fy_h, fz_h, cot_h, adj_o, gx_o, gy_o, gz_o,
               u, p, fx, fy, fz, rd, rhs, d, cb, adj, z, gx, gy, gz, db, raw,
               in_sem, out_sem, send_sem, recv_sem, edge_send, edge_recv):
        me = lax.axis_index("gx")
        core = me % 2
        near, far = me + 1 - 2 * core, me - 1 + 2 * core
        near_layer, far_layer = top - (top - 1) * core, 1 + (top - 1) * core
        near_halo, far_halo = high * (1 - core), high * core
        has_far = jnp.logical_and(far >= 0, far < n)
        has_below, has_above = me > 0, me < n - 1
        data = pl.ds(PAD, ny)

        loads = [
            pltpu.make_async_copy(saved_h, raw, in_sem.at[0]),
            pltpu.make_async_copy(fx_h, fx.at[pl.ds(0, layers)], in_sem.at[1]),
            pltpu.make_async_copy(cot_h, adj, in_sem.at[2]),
            pltpu.make_async_copy(fy_h, fy.at[:, data], in_sem.at[3]),
            pltpu.make_async_copy(fz_h, fz, in_sem.at[4]),
            pltpu.make_async_copy(rhs_h, rhs, in_sem.at[5]),
        ]
        for load in loads:
            load.start()

        barrier = pltpu.get_barrier_semaphore()
        pl.semaphore_signal(barrier, inc=1, device_id={"gx": near},
                            device_id_type=pl.DeviceIdType.MESH)

        @pl.when(has_far)
        def _():
            pl.semaphore_signal(barrier, inc=1, device_id={"gx": far},
                                device_id_type=pl.DeviceIdType.MESH)

        def halo(buf, which, k, side):
            layer, there, device = (
                (near_layer, high - near_halo, near) if side == 0
                else (far_layer, high - far_halo, far)
            )
            return pltpu.make_async_remote_copy(
                src_ref=buf.at[k, layer, data],
                dst_ref=buf.at[k, there, data],
                send_sem=send_sem.at[which, k, side],
                recv_sem=recv_sem.at[which, k, side],
                device_id={"gx": device},
                device_id_type=pl.DeviceIdType.MESH,
            )

        def on_side(side, action):
            if side == 0:
                action()
            else:
                pl.when(has_far)(action)

        def send(buf, which, k, side):
            on_side(side, lambda: halo(buf, which, k, side).start())

        def receive(buf, which, k, side):
            on_side(side, lambda: halo(buf, which, k, side).wait_recv())

        face_copy = pltpu.make_async_remote_copy(
            src_ref=fx.at[0], dst_ref=fx.at[layers],
            send_sem=edge_send.at[0], recv_sem=edge_recv.at[0],
            device_id={"gx": me - 1}, device_id_type=pl.DeviceIdType.MESH)
        diag_copy = pltpu.make_async_remote_copy(
            src_ref=db.at[top, data], dst_ref=db.at[0, data],
            send_sem=edge_send.at[1], recv_sem=edge_recv.at[1],
            device_id={"gx": me + 1}, device_id_type=pl.DeviceIdType.MESH)

        strip = jnp.zeros((PAD, nz), f32)

        def clear_pads(l, carry):
            for k in range(STEPS):
                for buf in (u, p):
                    buf[k, l + 1, pl.ds(0, PAD), :] = strip
                    buf[k, l + 1, pl.ds(PAD + ny, PAD), :] = strip
            fy[l, pl.ds(PAD + ny, PAD), :] = strip
            db[l + 1, pl.ds(0, PAD), :] = strip
            return carry

        lax.fori_loop(0, layers, clear_pads, 0)

        @pl.when(jnp.logical_not(has_far))
        def _():
            def clear(r, carry):
                for k in range(STEPS):
                    for buf in (u, p):
                        buf[k, far_halo, pl.ds(PAD + r * PAD, PAD), :] = strip
                return carry

            lax.fori_loop(0, ny // PAD, clear, 0)

        @pl.when(jnp.logical_not(has_above))
        def _():
            def clear(r, carry):
                fx[layers, pl.ds(r * PAD, PAD), :] = strip
                return carry

            lax.fori_loop(0, ny // PAD, clear, 0)

        @pl.when(jnp.logical_not(has_below))
        def _():
            def clear(r, carry):
                db[0, pl.ds(PAD + r * PAD, PAD), :] = strip
                return carry

            lax.fori_loop(0, ny // PAD, clear, 0)

        lane = lax.broadcasted_iota(jnp.int32, (ROWS, nz), 1)
        first_lane, last_lane = lane == 0, lane == nz - 1

        def lower_z(x):
            return jnp.where(first_lane, 0.0, pltpu.roll(x, 1, 1))

        def upper_z(x):
            return jnp.where(last_lane, 0.0, pltpu.roll(x, nz - 1, 1))

        def lower_y(load, r):
            tall = load(pl.ds(pl.multiple_of(r, PAD), ROWS + PAD))
            return pltpu.roll(tall, 1, 0)[PAD:]

        def upper_y(load, r):
            tall = load(pl.ds(pl.multiple_of(PAD + r, PAD), ROWS + PAD))
            return pltpu.roll(tall, ROWS + PAD - 1, 0)[:ROWS]

        def over_rows(body):
            def step(i, carry):
                body(pl.multiple_of(i * ROWS, ROWS))
                return carry

            lax.fori_loop(0, ny // ROWS, step, 0)

        def stencil(buf, k, l, r):
            here = buf[k, l, pl.ds(PAD + r, ROWS), :]
            flow = fx[l - 1, pl.ds(r, ROWS), :] * (here - buf[k, l - 1, pl.ds(PAD + r, ROWS), :])
            flow += fx[l, pl.ds(r, ROWS), :] * (here - buf[k, l + 1, pl.ds(PAD + r, ROWS), :])
            flow += fy[l - 1, pl.ds(PAD + r, ROWS), :] * (
                here - lower_y(lambda i: buf[k, l, i, :], r))
            flow += upper_y(lambda i: fy[l - 1, i, :], r) * (
                here - upper_y(lambda i: buf[k, l, i, :], r))
            along = fz[l - 1, pl.ds(r, ROWS), :] * (here - lower_z(here))
            return here, flow + (along - upper_z(along))

        def widen(l):
            def body(r):
                u[0, l, pl.ds(PAD + r, ROWS), :] = raw[l - 1, pl.ds(r, ROWS), :].astype(f32)

            over_rows(body)

        def prepare(l):
            def body(r):
                rows = pl.ds(r, ROWS)
                across = fz[l - 1, rows, :]
                diagonal = (
                    fx[l - 1, rows, :] + fx[l, rows, :]
                    + fy[l - 1, pl.ds(PAD + r, ROWS), :]
                    + upper_y(lambda i: fy[l - 1, i, :], r)
                    + across + upper_z(across)
                )
                inverse = 1.0 / diagonal
                rd[l - 1, rows, :] = inverse
                seed = adj[l - 1, rows, :]
                cb[l - 1, rows, :] = seed
                p[last, l, pl.ds(PAD + r, ROWS), :] = (-coefs[last][1]) * seed * inverse

            over_rows(body)

        def forward(k, l):
            def body(r):
                rows = pl.ds(r, ROWS)
                here, flow = stencil(u, k, l, r)
                scaled = (rhs[l - 1, rows, :] - flow) * rd[l - 1, rows, :]
                z[k, l - 1, rows, :] = scaled
                if k < last:
                    change = coefs[k][1] * scaled
                    if k > 0:
                        change += coefs[k][0] * d[l - 1, rows, :]
                    d[l - 1, rows, :] = change
                    u[k + 1, l, pl.ds(PAD + r, ROWS), :] = here + change

            over_rows(body)

        def backward(k, l):
            def body(r):
                rows = pl.ds(r, ROWS)
                here, flow = stencil(p, k, l, r)
                total = adj[l - 1, rows, :] + flow
                adj[l - 1, rows, :] = total
                if k > 0:
                    change = total + coefs[k][0] * cb[l - 1, rows, :]
                    cb[l - 1, rows, :] = change
                    p[k - 1, l, pl.ds(PAD + r, ROWS), :] = (
                        (-coefs[k - 1][1]) * change * rd[l - 1, rows, :])

            over_rows(body)

        def grads(l, r, steps):
            sums = [None, None, None]
            for k in steps:
                mine = pl.ds(PAD + r, ROWS)
                a, b = u[k, l, mine, :], p[k, l, mine, :]
                terms = (
                    (a - u[k, l - 1, mine, :]) * (b - p[k, l - 1, mine, :]),
                    (a - lower_y(lambda i: u[k, l, i, :], r))
                    * (b - lower_y(lambda i: p[k, l, i, :], r)),
                    (a - lower_z(a)) * (b - lower_z(b)),
                )
                sums = [t if s is None else s + t for s, t in zip(sums, terms)]
            return sums

        def middle_grads(l):
            def body(r):
                rows = pl.ds(r, ROWS)
                for out, value in zip((gx, gy, gz), grads(l, r, (1, 2))):
                    out[l - 1, rows, :] = value

            over_rows(body)

        def diag_bar(l):
            def body(r):
                mine = pl.ds(PAD + r, ROWS)
                total = p[0, l, mine, :] * z[0, l - 1, pl.ds(r, ROWS), :]
                for k in range(1, STEPS):
                    total += p[k, l, mine, :] * z[k, l - 1, pl.ds(r, ROWS), :]
                db[l, mine, :] = total

            over_rows(body)

        def end_grads(l):
            def body(r):
                rows, mine = pl.ds(r, ROWS), pl.ds(PAD + r, ROWS)
                x, y, across = grads(l, r, (0, last))
                extra = db[l, mine, :]
                gx[l - 1, rows, :] += x + (extra + db[l - 1, mine, :])
                gy[l - 1, rows, :] += y + (extra + lower_y(lambda i: db[l, i, :], r))
                gz[l - 1, rows, :] += across + (extra + lower_z(extra))

            over_rows(body)

        def each_layer(first, end, action):
            def step(l, carry):
                action(l)
                return carry

            lax.fori_loop(first, end, step, 0)

        outs = ((adj, adj_o), (gx, gx_o), (gy, gy_o), (gz, gz_o))

        def stores(l, which):
            return [
                pltpu.make_async_copy(
                    outs[i][0].at[l - 1], outs[i][1].at[l - 1], out_sem.at[i, l - 1])
                for i in which
            ]

        loads[0].wait()
        each_layer(1, top + 1, widen)
        @pl.when(has_far)
        def _():
            pl.semaphore_wait(barrier, 2)

        @pl.when(jnp.logical_not(has_far))
        def _():
            pl.semaphore_wait(barrier, 1)

        loads[1].wait()
        pl.when(has_below)(face_copy.start)
        send(u, 0, 0, 0)
        send(u, 0, 0, 1)
        for load in loads[2:5]:
            load.wait()
        each_layer(1, top, prepare)
        pl.when(has_above)(face_copy.wait_recv)
        prepare(top)
        send(p, 1, last, 0)
        send(p, 1, last, 1)
        loads[5].wait()

        for k in range(last):
            back = last - k
            each_layer(2, top, lambda l: forward(k, l))
            for side, layer in ((0, near_layer), (1, far_layer)):
                receive(u, 0, k, side)
                forward(k, layer)
                send(u, 0, k + 1, side)
            each_layer(2, top, lambda l: backward(back, l))
            for side, layer in ((0, near_layer), (1, far_layer)):
                receive(p, 1, back, side)
                backward(back, layer)
                send(p, 1, back - 1, side)

        each_layer(2, top, lambda l: forward(last, l))
        each_layer(2, top, lambda l: backward(0, l))
        each_layer(1, top + 1, middle_grads)
        for side, layer in ((0, near_layer), (1, far_layer)):
            receive(u, 0, last, side)
            forward(last, layer)
        diag_bar(top)
        pl.when(has_above)(diag_copy.start)
        each_layer(1, top, diag_bar)
        each_layer(2, top + 1, end_grads)
        for l in range(2, top + 1):
            for store in stores(l, (1, 2, 3)):
                store.start()
        for side, layer in ((0, near_layer), (1, far_layer)):
            receive(p, 1, 0, side)
            backward(0, layer)
        for l in range(1, top + 1):
            stores(l, (0,))[0].start()
        pl.when(has_below)(diag_copy.wait_recv)
        end_grads(1)
        for store in stores(1, (1, 2, 3)):
            store.start()

        for which, buf in ((0, u), (1, p)):
            for k in range(STEPS):
                for side in range(2):
                    on_side(side, lambda: halo(buf, which, k, side).wait_send())
        pl.when(has_below)(face_copy.wait_send)
        pl.when(has_above)(diag_copy.wait_send)
        for l in range(1, top + 1):
            for store in stores(l, range(4)):
                store.wait()

    return kernel


def per_device(saved_field, right_side, face_x, face_y, face_z, cotangent):
    layers, ny, nz = face_x.shape
    n = lax.axis_size("gx")
    block = (layers, ny, nz)
    tall = ny + 2 * PAD

    def vmem(shape, dtype=jnp.float32):
        return pltpu.VMEM(shape, dtype)

    out = jax.ShapeDtypeStruct(block, jnp.float32)
    return pl.pallas_call(
        make_kernel(n, layers, ny, nz),
        out_shape=(out,) * 4,
        in_specs=[pl.BlockSpec(memory_space=pl.ANY)] * 6,
        out_specs=[pl.BlockSpec(memory_space=pl.ANY)] * 4,
        scratch_shapes=[
            vmem((STEPS, layers + 2, tall, nz)),
            vmem((STEPS, layers + 2, tall, nz)),
            vmem((layers + 1, ny, nz)),
            vmem((layers, tall, nz)),
            vmem(block),
            vmem(block),
            vmem(block),
            vmem(block),
            vmem(block),
            vmem(block),
            vmem((STEPS,) + block),
            vmem(block), vmem(block), vmem(block),
            vmem((layers + 1, tall, nz)),
            vmem(block, jnp.bfloat16),
            pltpu.SemaphoreType.DMA((6,)),
            pltpu.SemaphoreType.DMA((4, layers)),
            pltpu.SemaphoreType.DMA((2, STEPS, 2)),
            pltpu.SemaphoreType.DMA((2, STEPS, 2)),
            pltpu.SemaphoreType.DMA((2,)),
            pltpu.SemaphoreType.DMA((2,)),
        ],
        compiler_params=pltpu.CompilerParams(
            collective_id=0, has_side_effects=True, vmem_limit_bytes=48 * 1024 * 1024
        ),
        cost_estimate=pl.CostEstimate(
            flops=300 * layers * ny * nz, bytes_accessed=38 * layers * ny * nz, transcendentals=0
        ),
    )(saved_field, right_side, face_x, face_y, face_z, cotangent)


def solution(mesh):
    spec = P(("grp", "gx"), None, None)
    return jax.shard_map(
        per_device, mesh=mesh, in_specs=(spec,) * 6, out_specs=(spec,) * 4, check_vma=False
    )
```

profile of v0, /device:TPU:12, one launch (start us, length us, event | category | flops | bytes accessed | tf_op | source)
XLA Modules:
  0.0 72.0 jit_solution(2170115524610946298)
XLA Ops:
  0.6 0.0 copy-start
  0.6 1.2 %copy-done = f32[4,128,512]{2,1,0:T(8,128)S(1)} copy-done((f32[4,128,512]{2,1,0:T(8,128)S(1)}, f32[4,128,512]{2,1,0:T(8,128)}, u32[]{:S(2)}) %copy-start) | copy-done | bytes 1048600
  1.9 0.0 copy-start.1
  1.9 1.0 %copy-done.1 = bf16[4,128,512]{2,1,0:T(8,128)(2,1)S(1)} copy-done((bf16[4,128,512]{2,1,0:T(8,128)(2,1)S(1)}, bf16[4,128,512]{2,1,0:T(8,128)(2,1)}, u32[]{:S(2)}) %copy-start.1) | copy-done | bytes 524312
  2.9 65.2 %shard_map.93 = (f32[4,128,512]{2,1,0:T(8,128)S(1)}, f32[4,128,512]{2,1,0:T(8,128)S(1)}, f32[4,128,512]{2,1,0:T(8,128)S(1)}, f32[4,128,512]{2,1,0:T(8,128)S(1)}) custom-call(bf16[4,128,512]{2,1,0:T(8,128)(2,1)S(1)} %copy-done.1, f32[4,128,512]{2,1,0:T(8,128)S(1)} %copy-done, f32[4,128,512]{2,1,0:T(8,128)} %fx_h.1, f32[4,128,512]{2,1,0:T(8,128)} %fy_h.1, ...), custom_call_target="tpu_custom_call" | custom-call | flops 78643200 | bytes 9961472 | tf_op jit(solution)/shard_map/pallas_call | solution.py:371
  68.1 1.0 %copy.14 = f32[4,128,512]{2,1,0:T(8,128)} copy(f32[4,128,512]{2,1,0:T(8,128)S(1)} %get-tuple-element.8) | data formatting | bytes 2097152
  69.1 1.0 %copy.15 = f32[4,128,512]{2,1,0:T(8,128)} copy(f32[4,128,512]{2,1,0:T(8,128)S(1)} %get-tuple-element.9) | data formatting | bytes 2097152
  70.0 1.0 %copy.16 = f32[4,128,512]{2,1,0:T(8,128)} copy(f32[4,128,512]{2,1,0:T(8,128)S(1)} %get-tuple-element.10) | data formatting | bytes 2097152
  71.0 1.0 %copy.17 = f32[4,128,512]{2,1,0:T(8,128)} copy(f32[4,128,512]{2,1,0:T(8,128)S(1)} %get-tuple-element.11) | data formatting | bytes 2097152
Async XLA Ops:
  0.6 1.2 %copy-start = (f32[4,128,512]{2,1,0:T(8,128)S(1)}, f32[4,128,512]{2,1,0:T(8,128)}, u32[]{:S(2)}) copy-start(f32[4,128,512]{2,1,0:T(8,128)} %rhs_h.1) | copy-start | bytes 3145732
  1.9 1.0 %copy-start.1 = (bf16[4,128,512]{2,1,0:T(8,128)(2,1)S(1)}, bf16[4,128,512]{2,1,0:T(8,128)(2,1)}, u32[]{:S(2)}) copy-start(bf16[4,128,512]{2,1,0:T(8,128)(2,1)} %saved_h.1) | copy-start | bytes 1572868
where the time goes:
time: 73.1 us; the launch traced here: 72 us
  Pallas kernels  65.2 us (89%)
  local copies, waits for them, and re-layouts  6.14 us (8%)
    pallas_call x1, Pallas kernels, per_device(): pl.pallas_call(make_kernel(n, layers, ny, nz), out_shape=(out,) * 4, in_s...  65.2 us
    unnamed x8, local copies, waits for them, and re-layouts  6.14 us

commit v1 on v0

v1 whole, which is shorter than its diff:
```python
import jax
import jax.numpy as jnp
from jax import lax
from jax.experimental import pallas as pl
from jax.experimental.pallas import tpu as pltpu
from jax.sharding import PartitionSpec as P

STEPS = 4
ROWS = 64
PAD = 8

spectrum_low = 0.25
spectrum_high = 2.05


def chebyshev(count):
    centre = (spectrum_high + spectrum_low) / 2.0
    half = (spectrum_high - spectrum_low) / 2.0
    ratio = centre / half
    rho_prev = 1.0 / ratio
    coefs = [(0.0, 1.0 / centre)]
    for index in range(1, count):
        rho_next = 1.0 / (2.0 * ratio - rho_prev)
        coefs.append((rho_next * rho_prev, 2.0 * rho_next / half))
        rho_prev = rho_next
    return coefs


def make_kernel(n, layers, ny, nz):
    coefs = chebyshev(STEPS)
    top = layers
    high = layers + 1
    last = STEPS - 1
    f32 = jnp.float32

    def kernel(saved_h, rhs_h, fx_h, fy_h, fz_h, cot_h, adj_o, gx_o, gy_o, gz_o,
               u, p, fx, fy, fz, rd, rhs, d, cb, adj, z, gx, gy, gz, db, raw,
               in_sem, out_sem, send_sem, recv_sem, edge_send, edge_recv,
               diag_send, diag_recv):
        me = lax.axis_index("gx")
        core = me % 2
        near, far = me + 1 - 2 * core, me - 1 + 2 * core
        near_layer, far_layer = top - (top - 1) * core, 1 + (top - 1) * core
        near_halo, far_halo = high * (1 - core), high * core
        has_far = jnp.logical_and(far >= 0, far < n)
        has_below, has_above = me > 0, me < n - 1
        data = pl.ds(PAD, ny)

        loads = [
            pltpu.make_async_copy(saved_h, raw, in_sem.at[0]),
            pltpu.make_async_copy(fx_h, fx.at[pl.ds(0, layers)], in_sem.at[1]),
            pltpu.make_async_copy(cot_h, adj, in_sem.at[2]),
            pltpu.make_async_copy(fy_h, fy.at[:, data], in_sem.at[3]),
            pltpu.make_async_copy(fz_h, fz, in_sem.at[4]),
            pltpu.make_async_copy(rhs_h, rhs, in_sem.at[5]),
        ]
        for load in loads:
            load.start()

        barrier = pltpu.get_barrier_semaphore()
        pl.semaphore_signal(barrier, inc=1, device_id={"gx": near},
                            device_id_type=pl.DeviceIdType.MESH)

        @pl.when(has_far)
        def _():
            pl.semaphore_signal(barrier, inc=1, device_id={"gx": far},
                                device_id_type=pl.DeviceIdType.MESH)

        def halo(buf, which, k, side, c):
            layer, there, device = (
                (near_layer, high - near_halo, near) if side == 0
                else (far_layer, high - far_halo, far)
            )
            part = pl.ds(pl.multiple_of(PAD + c * ROWS, PAD), ROWS)
            return pltpu.make_async_remote_copy(
                src_ref=buf.at[k, layer, part],
                dst_ref=buf.at[k, there, part],
                send_sem=send_sem.at[which, k, side, c],
                recv_sem=recv_sem.at[which, k, side, c],
                device_id={"gx": device},
                device_id_type=pl.DeviceIdType.MESH,
            )

        def on_side(side, action):
            if side == 0:
                action()
            else:
                pl.when(has_far)(action)

        chunks = ny // ROWS

        def send(buf, which, k, side, c):
            on_side(side, lambda: halo(buf, which, k, side, c).start())

        def receive(buf, which, k, side, c):
            on_side(side, lambda: halo(buf, which, k, side, c).wait_recv())

        def each(first, end, action):
            def step(i, carry):
                action(i)
                return carry

            lax.fori_loop(first, end, step, 0)

        face_copy = pltpu.make_async_remote_copy(
            src_ref=fx.at[0], dst_ref=fx.at[layers],
            send_sem=edge_send.at[0], recv_sem=edge_recv.at[0],
            device_id={"gx": me - 1}, device_id_type=pl.DeviceIdType.MESH)
        def diag_copy(c):
            part = pl.ds(pl.multiple_of(PAD + c * ROWS, PAD), ROWS)
            return pltpu.make_async_remote_copy(
                src_ref=db.at[top, part], dst_ref=db.at[0, part],
                send_sem=diag_send.at[c], recv_sem=diag_recv.at[c],
                device_id={"gx": me + 1}, device_id_type=pl.DeviceIdType.MESH)

        strip = jnp.zeros((PAD, nz), f32)

        def clear_pads(l, carry):
            for k in range(STEPS):
                for buf in (u, p):
                    buf[k, l + 1, pl.ds(0, PAD), :] = strip
                    buf[k, l + 1, pl.ds(PAD + ny, PAD), :] = strip
            fy[l, pl.ds(PAD + ny, PAD), :] = strip
            db[l + 1, pl.ds(0, PAD), :] = strip
            return carry

        lax.fori_loop(0, layers, clear_pads, 0)

        @pl.when(jnp.logical_not(has_far))
        def _():
            def clear(r, carry):
                for k in range(STEPS):
                    for buf in (u, p):
                        buf[k, far_halo, pl.ds(PAD + r * PAD, PAD), :] = strip
                return carry

            lax.fori_loop(0, ny // PAD, clear, 0)

        @pl.when(jnp.logical_not(has_above))
        def _():
            def clear(r, carry):
                fx[layers, pl.ds(r * PAD, PAD), :] = strip
                return carry

            lax.fori_loop(0, ny // PAD, clear, 0)

        @pl.when(jnp.logical_not(has_below))
        def _():
            def clear(r, carry):
                db[0, pl.ds(PAD + r * PAD, PAD), :] = strip
                return carry

            lax.fori_loop(0, ny // PAD, clear, 0)

        lane = lax.broadcasted_iota(jnp.int32, (ROWS, nz), 1)
        first_lane, last_lane = lane == 0, lane == nz - 1

        def lower_z(x):
            return jnp.where(first_lane, 0.0, pltpu.roll(x, 1, 1))

        def upper_z(x):
            return jnp.where(last_lane, 0.0, pltpu.roll(x, nz - 1, 1))

        def lower_y(load, r):
            tall = load(pl.ds(pl.multiple_of(r, PAD), ROWS + PAD))
            return pltpu.roll(tall, 1, 0)[PAD:]

        def upper_y(load, r):
            tall = load(pl.ds(pl.multiple_of(PAD + r, PAD), ROWS + PAD))
            return pltpu.roll(tall, ROWS + PAD - 1, 0)[:ROWS]

        def over_rows(body, l):
            each(0, chunks, lambda c: body(l, pl.multiple_of(c * ROWS, ROWS), c))

        def stencil(buf, k, l, r):
            here = buf[k, l, pl.ds(PAD + r, ROWS), :]
            flow = fx[l - 1, pl.ds(r, ROWS), :] * (here - buf[k, l - 1, pl.ds(PAD + r, ROWS), :])
            flow += fx[l, pl.ds(r, ROWS), :] * (here - buf[k, l + 1, pl.ds(PAD + r, ROWS), :])
            flow += fy[l - 1, pl.ds(PAD + r, ROWS), :] * (
                here - lower_y(lambda i: buf[k, l, i, :], r))
            flow += upper_y(lambda i: fy[l - 1, i, :], r) * (
                here - upper_y(lambda i: buf[k, l, i, :], r))
            along = fz[l - 1, pl.ds(r, ROWS), :] * (here - lower_z(here))
            return here, flow + (along - upper_z(along))

        def widen(l, r):
            u[0, l, pl.ds(PAD + r, ROWS), :] = raw[l - 1, pl.ds(r, ROWS), :].astype(f32)

        def prepare(l, r):
            rows = pl.ds(r, ROWS)
            across = fz[l - 1, rows, :]
            diagonal = (
                fx[l - 1, rows, :] + fx[l, rows, :]
                + fy[l - 1, pl.ds(PAD + r, ROWS), :]
                + upper_y(lambda i: fy[l - 1, i, :], r)
                + across + upper_z(across)
            )
            inverse = 1.0 / diagonal
            rd[l - 1, rows, :] = inverse
            seed = adj[l - 1, rows, :]
            cb[l - 1, rows, :] = seed
            p[last, l, pl.ds(PAD + r, ROWS), :] = (-coefs[last][1]) * seed * inverse

        def forward(k, l, r):
            rows = pl.ds(r, ROWS)
            here, flow = stencil(u, k, l, r)
            scaled = (rhs[l - 1, rows, :] - flow) * rd[l - 1, rows, :]
            z[k, l - 1, rows, :] = scaled
            if k < last:
                change = coefs[k][1] * scaled
                if k > 0:
                    change += coefs[k][0] * d[l - 1, rows, :]
                d[l - 1, rows, :] = change
                u[k + 1, l, pl.ds(PAD + r, ROWS), :] = here + change

        def backward(k, l, r):
            rows = pl.ds(r, ROWS)
            here, flow = stencil(p, k, l, r)
            total = adj[l - 1, rows, :] + flow
            adj[l - 1, rows, :] = total
            if k > 0:
                change = total + coefs[k][0] * cb[l - 1, rows, :]
                cb[l - 1, rows, :] = change
                p[k - 1, l, pl.ds(PAD + r, ROWS), :] = (
                    (-coefs[k - 1][1]) * change * rd[l - 1, rows, :])

        def grads(l, r, steps):
            sums = [None, None, None]
            for k in steps:
                mine = pl.ds(PAD + r, ROWS)
                a, b = u[k, l, mine, :], p[k, l, mine, :]
                terms = (
                    (a - u[k, l - 1, mine, :]) * (b - p[k, l - 1, mine, :]),
                    (a - lower_y(lambda i: u[k, l, i, :], r))
                    * (b - lower_y(lambda i: p[k, l, i, :], r)),
                    (a - lower_z(a)) * (b - lower_z(b)),
                )
                sums = [t if s is None else s + t for s, t in zip(sums, terms)]
            return sums

        def middle_grads(l, r):
            rows = pl.ds(r, ROWS)
            for out, value in zip((gx, gy, gz), grads(l, r, (1, 2))):
                out[l - 1, rows, :] = value

        def diag_bar(l, r):
            mine = pl.ds(PAD + r, ROWS)
            total = p[0, l, mine, :] * z[0, l - 1, pl.ds(r, ROWS), :]
            for k in range(1, STEPS):
                total += p[k, l, mine, :] * z[k, l - 1, pl.ds(r, ROWS), :]
            db[l, mine, :] = total

        def end_grads(l, r):
            rows, mine = pl.ds(r, ROWS), pl.ds(PAD + r, ROWS)
            x, y, across = grads(l, r, (0, last))
            extra = db[l, mine, :]
            gx[l - 1, rows, :] += x + (extra + db[l - 1, mine, :])
            gy[l - 1, rows, :] += y + (extra + lower_y(lambda i: db[l, i, :], r))
            gz[l - 1, rows, :] += across + (extra + lower_z(extra))

        def rows_of(action, l):
            each(0, chunks, lambda c: action(l, pl.multiple_of(c * ROWS, ROWS)))

        def layers_of(first, end, action):
            each(first, end, lambda l: rows_of(action, l))

        def first_send(buf, which, k):
            for side in range(2):
                each(0, chunks, lambda c: send(buf, which, k, side, c))

        outs = ((adj, adj_o), (gx, gx_o), (gy, gy_o), (gz, gz_o))

        def stores(l, which):
            return [
                pltpu.make_async_copy(
                    outs[i][0].at[l - 1], outs[i][1].at[l - 1], out_sem.at[i, l - 1])
                for i in which
            ]

        loads[0].wait()
        layers_of(1, top + 1, widen)
        @pl.when(has_far)
        def _():
            pl.semaphore_wait(barrier, 2)

        @pl.when(jnp.logical_not(has_far))
        def _():
            pl.semaphore_wait(barrier, 1)

        loads[1].wait()
        pl.when(has_below)(face_copy.start)
        first_send(u, 0, 0)
        for load in loads[2:5]:
            load.wait()
        layers_of(1, top, prepare)
        pl.when(has_above)(face_copy.wait_recv)
        rows_of(prepare, top)
        first_send(p, 1, last)
        loads[5].wait()

        def halo_step(k, side, layer, buf, which, step, following):
            def chunk(c):
                receive(buf, which, k, side, c)
                step(k, layer, pl.multiple_of(c * ROWS, ROWS))
                if following is not None:
                    send(buf, which, following, side, c)

            each(0, chunks, chunk)

        for k in range(last):
            back = last - k
            layers_of(2, top, lambda l, r: forward(k, l, r))
            layers_of(2, top, lambda l, r: backward(back, l, r))
            for side, layer in ((0, near_layer), (1, far_layer)):
                halo_step(k, side, layer, u, 0, forward, k + 1)
                halo_step(back, side, layer, p, 1, backward, back - 1)

        def store(l, which):
            for copy in stores(l, which):
                copy.start()

        def finish(l):
            rows_of(end_grads, l)
            store(l, (1, 2, 3))

        def close(k, l, r):
            forward(k, l, r)
            diag_bar(l, r)

        def close_backward(l):
            store(l, (0,))

        layers_of(2, top, lambda l, r: close(last, l, r))
        layers_of(2, top, lambda l, r: backward(0, l, r))
        layers_of(1, top + 1, middle_grads)
        each(2, top, close_backward)
        halo_step(last, 0, near_layer, u, 0, close, None)

        @pl.when(jnp.logical_and(core == 0, has_above))
        def _():
            each(0, chunks, lambda c: diag_copy(c).start())

        halo_step(0, 0, near_layer, p, 1, backward, None)
        store(near_layer, (0,))
        each(3 - core, top + 1 - core, finish)

        def far_chunk(c):
            receive(u, 0, last, 1, c)
            close(last, far_layer, pl.multiple_of(c * ROWS, ROWS))

            @pl.when(jnp.logical_and(core == 1, has_above))
            def _():
                diag_copy(c).start()

        each(0, chunks, far_chunk)
        finish(2 + (top - 2) * core)
        halo_step(0, 1, far_layer, p, 1, backward, None)
        store(far_layer, (0,))

        def last_chunk(c):
            @pl.when(has_below)
            def _():
                diag_copy(c).wait_recv()

            end_grads(1, pl.multiple_of(c * ROWS, ROWS))

        each(0, chunks, last_chunk)
        store(1, (1, 2, 3))

        for which, buf in ((0, u), (1, p)):
            for k in range(STEPS):
                for side in range(2):
                    each(0, chunks, lambda c: on_side(
                        side, lambda: halo(buf, which, k, side, c).wait_send()))
        pl.when(has_below)(face_copy.wait_send)

        @pl.when(has_above)
        def _():
            each(0, chunks, lambda c: diag_copy(c).wait_send())

        def wait_stores(l):
            for copy in stores(l, range(4)):
                copy.wait()

        each(1, top + 1, wait_stores)

    return kernel


def per_device(saved_field, right_side, face_x, face_y, face_z, cotangent):
    layers, ny, nz = face_x.shape
    n = lax.axis_size("gx")
    block = (layers, ny, nz)
    tall = ny + 2 * PAD

    def vmem(shape, dtype=jnp.float32):
        return pltpu.VMEM(shape, dtype)

    out = jax.ShapeDtypeStruct(block, jnp.float32)
    return pl.pallas_call(
        make_kernel(n, layers, ny, nz),
        out_shape=(out,) * 4,
        in_specs=[pl.BlockSpec(memory_space=pl.ANY)] * 6,
        out_specs=[pl.BlockSpec(memory_space=pl.ANY)] * 4,
        scratch_shapes=[
            vmem((STEPS, layers + 2, tall, nz)),
            vmem((STEPS, layers + 2, tall, nz)),
            vmem((layers + 1, ny, nz)),
            vmem((layers, tall, nz)),
            vmem(block),
            vmem(block),
            vmem(block),
            vmem(block),
            vmem(block),
            vmem(block),
            vmem((STEPS,) + block),
            vmem(block), vmem(block), vmem(block),
            vmem((layers + 1, tall, nz)),
            vmem(block, jnp.bfloat16),
            pltpu.SemaphoreType.DMA((6,)),
            pltpu.SemaphoreType.DMA((4, layers)),
            pltpu.SemaphoreType.DMA((2, STEPS, 2, ny // ROWS)),
            pltpu.SemaphoreType.DMA((2, STEPS, 2, ny // ROWS)),
            pltpu.SemaphoreType.DMA((1,)),
            pltpu.SemaphoreType.DMA((1,)),
            pltpu.SemaphoreType.DMA((ny // ROWS,)),
            pltpu.SemaphoreType.DMA((ny // ROWS,)),
        ],
        compiler_params=pltpu.CompilerParams(
            collective_id=0, has_side_effects=True, vmem_limit_bytes=60 * 1024 * 1024
        ),
        cost_estimate=pl.CostEstimate(
            flops=300 * layers * ny * nz, bytes_accessed=38 * layers * ny * nz, transcendentals=0
        ),
    )(saved_field, right_side, face_x, face_y, face_z, cotangent)


def solution(mesh):
    spec = P(("grp", "gx"), None, None)
    return jax.shard_map(
        per_device, mesh=mesh, in_specs=(spec,) * 6, out_specs=(spec,) * 4, check_vma=False
    )
```

time: 73.1 us -> 68.7 us (0.940); the launches traced: 72 us -> 68.4 us
  Pallas kernels: 65.2 us -> 61.2 us
    pallas_call x1, Pallas kernels: 65.2 us -> 61.2 us  [per_device(): pl.pallas_call(make_kernel(n, layers, ny, nz), out_shape=(out,) * 4, in_s...]
    unnamed x8 -> x10, local copies, waits for them, and re-layouts: 6.14 us -> 6.53 us
where the time goes in v1:
time: 68.7 us; the launch traced here: 68.4 us
  Pallas kernels  61.2 us (89%)
  local copies, waits for them, and re-layouts  6.53 us (10%)
    pallas_call x1, Pallas kernels, per_device(): pl.pallas_call(make_kernel(n, layers, ny, nz), out_shape=(out,) * 4, in_s...  61.2 us
    unnamed x10, local copies, waits for them, and re-layouts  6.53 us

profile of v1, /device:TPU:12, one launch (start us, length us, event | category | flops | bytes accessed | tf_op | source)
XLA Modules:
  0.0 68.4 jit_solution(1131259180071763781)
XLA Ops:
  0.6 61.2 %shard_map.93 = (f32[4,128,512]{2,1,0:T(8,128)}, f32[4,128,512]{2,1,0:T(8,128)}, f32[4,128,512]{2,1,0:T(8,128)}, f32[4,128,512]{2,1,0:T(8,128)}) custom-call(bf16[4,128,512]{2,1,0:T(8,128)(2,1)} %saved_h.1, f32[4,128,512]{2,1,0:T(8,128)} %rhs_h.1, f32[4,128,512]{2,1,0:T(8,128)} %fx_h.1, f32[4,128,512]{2,1,0:T(8,128)} %fy_h.1, f32[4,128,512]{2,1,0:T(8,128)} %fz_h.1, ...), custom_call_target="tpu_custom_call" | custom-call | flops 78643200 | bytes 9961472 | tf_op jit(solution)/shard_map/pallas_call | solution.py:400
  61.9 0.0 copy-start.2
  61.9 2.4 %copy.14 = f32[4,128,512]{2,1,0:T(8,128)} copy(f32[4,128,512]{2,1,0:T(8,128)} %get-tuple-element.8) | data formatting | bytes 2097152
  64.2 0.0 copy-done.2
  64.2 0.0 copy-start.1
  64.2 1.0 %copy.15 = f32[4,128,512]{2,1,0:T(8,128)} copy(f32[4,128,512]{2,1,0:T(8,128)S(1)} %copy-done.2) | data formatting | bytes 2097152
  65.2 0.6 copy-done.1
  65.8 0.0 copy-start
  65.8 1.0 %copy.16 = f32[4,128,512]{2,1,0:T(8,128)} copy(f32[4,128,512]{2,1,0:T(8,128)S(1)} %copy-done.1) | data formatting | bytes 2097152
  66.8 0.6 copy-done
  67.4 1.0 %copy.17 = f32[4,128,512]{2,1,0:T(8,128)} copy(f32[4,128,512]{2,1,0:T(8,128)S(1)} %copy-done) | data formatting | bytes 2097152
Async XLA Ops:
  61.9 2.4 %copy-start.2 = (f32[4,128,512]{2,1,0:T(8,128)S(1)}, f32[4,128,512]{2,1,0:T(8,128)}, u32[]{:S(2)}) copy-start(f32[4,128,512]{2,1,0:T(8,128)} %get-tuple-element.9) | copy-start | bytes 3145732
  64.2 1.6 %copy-start.1 = (f32[4,128,512]{2,1,0:T(8,128)S(1)}, f32[4,128,512]{2,1,0:T(8,128)}, u32[]{:S(2)}) copy-start(f32[4,128,512]{2,1,0:T(8,128)} %get-tuple-element.10) | copy-start | bytes 3145732
  65.8 1.6 %copy-start = (f32[4,128,512]{2,1,0:T(8,128)S(1)}, f32[4,128,512]{2,1,0:T(8,128)}, u32[]{:S(2)}) copy-start(f32[4,128,512]{2,1,0:T(8,128)} %get-tuple-element.11) | copy-start | bytes 3145732

commit v2 on v1

--- a/solution.py
+++ b/solution.py
@@ -33,9 +33,9 @@
     last = STEPS - 1
     f32 = jnp.float32
 
-    def kernel(saved_h, rhs_h, fx_h, fy_h, fz_h, cot_h, adj_o, gx_o, gy_o, gz_o,
-               u, p, fx, fy, fz, rd, rhs, d, cb, adj, z, gx, gy, gz, db, raw,
-               in_sem, out_sem, send_sem, recv_sem, edge_send, edge_recv,
+    def kernel(saved_h, rhs_h, fx_h, fy_h, fz_h, cot_h, adj, gx, gy, gz,
+               u, p, fx, fy, fz, rd, rhs, d, cb, z, db, raw,
+               in_sem, send_sem, recv_sem, edge_send, edge_recv,
                diag_send, diag_recv):
         me = lax.axis_index("gx")
         core = me % 2
@@ -265,17 +265,8 @@
             each(first, end, lambda l: rows_of(action, l))
 
         def first_send(buf, which, k):
-            for side in range(2):
+            for side in (1, 0):
                 each(0, chunks, lambda c: send(buf, which, k, side, c))
-
-        outs = ((adj, adj_o), (gx, gx_o), (gy, gy_o), (gz, gz_o))
-
-        def stores(l, which):
-            return [
-                pltpu.make_async_copy(
-                    outs[i][0].at[l - 1], outs[i][1].at[l - 1], out_sem.at[i, l - 1])
-                for i in which
-            ]
 
         loads[0].wait()
         layers_of(1, top + 1, widen)
@@ -315,25 +306,16 @@
                 halo_step(k, side, layer, u, 0, forward, k + 1)
                 halo_step(back, side, layer, p, 1, backward, back - 1)
 
-        def store(l, which):
-            for copy in stores(l, which):
-                copy.start()
-
         def finish(l):
             rows_of(end_grads, l)
-            store(l, (1, 2, 3))
 
         def close(k, l, r):
             forward(k, l, r)
             diag_bar(l, r)
 
-        def close_backward(l):
-            store(l, (0,))
-
         layers_of(2, top, lambda l, r: close(last, l, r))
         layers_of(2, top, lambda l, r: backward(0, l, r))
         layers_of(1, top + 1, middle_grads)
-        each(2, top, close_backward)
         halo_step(last, 0, near_layer, u, 0, close, None)
 
         @pl.when(jnp.logical_and(core == 0, has_above))
@@ -341,7 +323,6 @@
             each(0, chunks, lambda c: diag_copy(c).start())
 
         halo_step(0, 0, near_layer, p, 1, backward, None)
-        store(near_layer, (0,))
         each(3 - core, top + 1 - core, finish)
 
         def far_chunk(c):
@@ -355,7 +336,6 @@
         each(0, chunks, far_chunk)
         finish(2 + (top - 2) * core)
         halo_step(0, 1, far_layer, p, 1, backward, None)
-        store(far_layer, (0,))
 
         def last_chunk(c):
             @pl.when(has_below)
@@ -365,7 +345,6 @@
             end_grads(1, pl.multiple_of(c * ROWS, ROWS))
 
         each(0, chunks, last_chunk)
-        store(1, (1, 2, 3))
 
         for which, buf in ((0, u), (1, p)):
             for k in range(STEPS):
@@ -378,12 +357,6 @@
         def _():
             each(0, chunks, lambda c: diag_copy(c).wait_send())
 
-        def wait_stores(l):
-            for copy in stores(l, range(4)):
-                copy.wait()
-
-        each(1, top + 1, wait_stores)
-
     return kernel
 
 
@@ -401,7 +374,7 @@
         make_kernel(n, layers, ny, nz),
         out_shape=(out,) * 4,
         in_specs=[pl.BlockSpec(memory_space=pl.ANY)] * 6,
-        out_specs=[pl.BlockSpec(memory_space=pl.ANY)] * 4,
+        out_specs=[pl.BlockSpec(memory_space=pltpu.VMEM)] * 4,
         scratch_shapes=[
             vmem((STEPS, layers + 2, tall, nz)),
             vmem((STEPS, layers + 2, tall, nz)),
@@ -412,13 +385,10 @@
             vmem(block),
             vmem(block),
             vmem(block),
-            vmem(block),
             vmem((STEPS,) + block),
-            vmem(block), vmem(block), vmem(block),
             vmem((layers + 1, tall, nz)),
             vmem(block, jnp.bfloat16),
             pltpu.SemaphoreType.DMA((6,)),
-            pltpu.SemaphoreType.DMA((4, layers)),
             pltpu.SemaphoreType.DMA((2, STEPS, 2, ny // ROWS)),
             pltpu.SemaphoreType.DMA((2, STEPS, 2, ny // ROWS)),
             pltpu.SemaphoreType.DMA((1,)),
@@ -427,7 +397,7 @@
             pltpu.SemaphoreType.DMA((ny // ROWS,)),
         ],
         compiler_params=pltpu.CompilerParams(
-            collective_id=0, has_side_effects=True, vmem_limit_bytes=60 * 1024 * 1024
+            collective_id=0, has_side_effects=True, vmem_limit_bytes=50 * 1024 * 1024
         ),
         cost_estimate=pl.CostEstimate(
             flops=300 * layers * ny * nz, bytes_accessed=38 * layers * ny * nz, transcendentals=0

time: 68.7 us -> 67.8 us (0.987)
  local copies, waits for them, and re-layouts: 6.53 us -> 5.55 us
    unnamed x10 -> x8, local copies, waits for them, and re-layouts: 6.53 us -> 5.55 us
where the time goes in v2:
time: 67.8 us; the launch traced here: 67.6 us
  Pallas kernels  61.4 us (91%)
  local copies, waits for them, and re-layouts  5.55 us (8%)
    pallas_call x1, Pallas kernels, per_device(): pl.pallas_call(make_kernel(n, layers, ny, nz), out_shape=(out,) * 4, in_s...  61.4 us
    unnamed x8, local copies, waits for them, and re-layouts  5.55 us

profile of v2, /device:TPU:12, one launch (start us, length us, event | category | flops | bytes accessed | tf_op | source)
XLA Modules:
  0.0 67.6 jit_solution(7615666066250598222)
XLA Ops:
  0.6 0.0 copy-start
  0.6 1.0 %copy-done = bf16[4,128,512]{2,1,0:T(8,128)(2,1)S(1)} copy-done((bf16[4,128,512]{2,1,0:T(8,128)(2,1)S(1)}, bf16[4,128,512]{2,1,0:T(8,128)(2,1)}, u32[]{:S(2)}) %copy-start) | copy-done | bytes 524312
  1.7 61.4 %shard_map.93 = (f32[4,128,512]{2,1,0:T(8,128)S(1)}, f32[4,128,512]{2,1,0:T(8,128)S(1)}, f32[4,128,512]{2,1,0:T(8,128)S(1)}, f32[4,128,512]{2,1,0:T(8,128)}) custom-call(bf16[4,128,512]{2,1,0:T(8,128)(2,1)S(1)} %copy-done, f32[4,128,512]{2,1,0:T(8,128)} %rhs_h.1, f32[4,128,512]{2,1,0:T(8,128)} %fx_h.1, f32[4,128,512]{2,1,0:T(8,128)} %fy_h.1, ...), custom_call_target="tpu_custom_call" | custom-call | flops 78643200 | bytes 9961472 | tf_op jit(solution)/shard_map/pallas_call | solution.py:373
  63.1 1.0 %copy.14 = f32[4,128,512]{2,1,0:T(8,128)} copy(f32[4,128,512]{2,1,0:T(8,128)S(1)} %get-tuple-element.8) | data formatting | bytes 2097152
  64.1 1.0 %copy.15 = f32[4,128,512]{2,1,0:T(8,128)} copy(f32[4,128,512]{2,1,0:T(8,128)S(1)} %get-tuple-element.9) | data formatting | bytes 2097152
  65.0 0.0 copy-start.1
  65.1 1.0 %copy.16 = f32[4,128,512]{2,1,0:T(8,128)} copy(f32[4,128,512]{2,1,0:T(8,128)S(1)} %get-tuple-element.10) | data formatting | bytes 2097152
  66.0 0.6 copy-done.1
  66.7 1.0 %copy.17 = f32[4,128,512]{2,1,0:T(8,128)} copy(f32[4,128,512]{2,1,0:T(8,128)S(1)} %copy-done.1) | data formatting | bytes 2097152
Async XLA Ops:
  0.6 1.0 %copy-start = (bf16[4,128,512]{2,1,0:T(8,128)(2,1)S(1)}, bf16[4,128,512]{2,1,0:T(8,128)(2,1)}, u32[]{:S(2)}) copy-start(bf16[4,128,512]{2,1,0:T(8,128)(2,1)} %saved_h.1) | copy-start | bytes 1572868
  65.0 1.6 %copy-start.1 = (f32[4,128,512]{2,1,0:T(8,128)S(1)}, f32[4,128,512]{2,1,0:T(8,128)}, u32[]{:S(2)}) copy-start(f32[4,128,512]{2,1,0:T(8,128)} %get-tuple-element.11) | copy-start | bytes 3145732

commit v3 on v2

--- a/solution.py
+++ b/solution.py
@@ -301,10 +301,11 @@
         for k in range(last):
             back = last - k
             layers_of(2, top, lambda l, r: forward(k, l, r))
+            halo_step(k, 0, near_layer, u, 0, forward, k + 1)
+            halo_step(k, 1, far_layer, u, 0, forward, k + 1)
             layers_of(2, top, lambda l, r: backward(back, l, r))
-            for side, layer in ((0, near_layer), (1, far_layer)):
-                halo_step(k, side, layer, u, 0, forward, k + 1)
-                halo_step(back, side, layer, p, 1, backward, back - 1)
+            halo_step(back, 0, near_layer, p, 1, backward, back - 1)
+            halo_step(back, 1, far_layer, p, 1, backward, back - 1)
 
         def finish(l):
             rows_of(end_grads, l)

time: 67.8 us -> 65 us (0.959)
  Pallas kernels: 61.4 us -> 58.6 us
    pallas_call x1, Pallas kernels: 61.4 us -> 58.6 us  [per_device(): pl.pallas_call(make_kernel(n, layers, ny, nz), out_shape=(out,) * 4, in_s...]
where the time goes in v3:
time: 65 us; the launch traced here: 64.8 us
  Pallas kernels  58.6 us (90%)
  local copies, waits for them, and re-layouts  5.55 us (9%)
  between operations  0.65 us (1%)
    pallas_call x1, Pallas kernels, per_device(): pl.pallas_call(make_kernel(n, layers, ny, nz), out_shape=(out,) * 4, in_s...  58.6 us
    unnamed x8, local copies, waits for them, and re-layouts  5.55 us

profile of v3, /device:TPU:12, one launch (start us, length us, event | category | flops | bytes accessed | tf_op | source)
XLA Modules:
  0.0 64.8 jit_solution(4126468726407788504)
XLA Ops:
  0.6 0.0 copy-start
  0.6 1.0 %copy-done = bf16[4,128,512]{2,1,0:T(8,128)(2,1)S(1)} copy-done((bf16[4,128,512]{2,1,0:T(8,128)(2,1)S(1)}, bf16[4,128,512]{2,1,0:T(8,128)(2,1)}, u32[]{:S(2)}) %copy-start) | copy-done | bytes 524312
  1.7 58.6 %shard_map.93 = (f32[4,128,512]{2,1,0:T(8,128)S(1)}, f32[4,128,512]{2,1,0:T(8,128)S(1)}, f32[4,128,512]{2,1,0:T(8,128)S(1)}, f32[4,128,512]{2,1,0:T(8,128)}) custom-call(bf16[4,128,512]{2,1,0:T(8,128)(2,1)S(1)} %copy-done, f32[4,128,512]{2,1,0:T(8,128)} %rhs_h.1, f32[4,128,512]{2,1,0:T(8,128)} %fx_h.1, f32[4,128,512]{2,1,0:T(8,128)} %fy_h.1, ...), custom_call_target="tpu_custom_call" | custom-call | flops 78643200 | bytes 9961472 | tf_op jit(solution)/shard_map/pallas_call | solution.py:374
  60.3 1.0 %copy.14 = f32[4,128,512]{2,1,0:T(8,128)} copy(f32[4,128,512]{2,1,0:T(8,128)S(1)} %get-tuple-element.8) | data formatting | bytes 2097152
  61.3 1.0 %copy.15 = f32[4,128,512]{2,1,0:T(8,128)} copy(f32[4,128,512]{2,1,0:T(8,128)S(1)} %get-tuple-element.9) | data formatting | bytes 2097152
  62.2 0.0 copy-start.1
  62.2 1.0 %copy.16 = f32[4,128,512]{2,1,0:T(8,128)} copy(f32[4,128,512]{2,1,0:T(8,128)S(1)} %get-tuple-element.10) | data formatting | bytes 2097152
  63.2 0.6 copy-done.1
  63.8 1.0 %copy.17 = f32[4,128,512]{2,1,0:T(8,128)} copy(f32[4,128,512]{2,1,0:T(8,128)S(1)} %copy-done.1) | data formatting | bytes 2097152
Async XLA Ops:
  0.6 1.0 %copy-start = (bf16[4,128,512]{2,1,0:T(8,128)(2,1)S(1)}, bf16[4,128,512]{2,1,0:T(8,128)(2,1)}, u32[]{:S(2)}) copy-start(bf16[4,128,512]{2,1,0:T(8,128)(2,1)} %saved_h.1) | copy-start | bytes 1572868
  62.2 1.6 %copy-start.1 = (f32[4,128,512]{2,1,0:T(8,128)S(1)}, f32[4,128,512]{2,1,0:T(8,128)}, u32[]{:S(2)}) copy-start(f32[4,128,512]{2,1,0:T(8,128)} %get-tuple-element.11) | copy-start | bytes 3145732
